TPU v7x, 32 devices: a whole 2x2x4 slice. The times are simulated.
32 devices in a mesh: grp: 2 (over y), clip: 4 (over z), head: 4 (over x, core).
Axes of the slice: x: 2, y: 2, z: 4, core: 2. Of those that a mesh axis runs over, the one named last changes fastest.
Arguments:
- pair_clips: int32 [32], P('grp'), parts along dimension 0, may hold values from 0 to 3, as said below
- pair_rows: bfloat16 [32, 32, 8, 1280], P(('grp', 'clip'), None, 'head'), parts along dimension 0, may hold values from -5 to 5
- prefix_kv: bfloat16 [8, 1024, 8, 256], P(('grp', 'clip'), None, 'head'), parts along dimension 0, may hold values from -4 to 4
Outputs:
- attended: bfloat16 [32, 32, 8, 1024], P(('grp', 'clip'), None, 'head'), parts along dimension 0
There are 2 independent parts, one for each index of `grp`. A program takes and returns all parts, laid end to end along the dimension named above; each array names one. Nothing has to cross between parts.
Inputs may be any that keep to these rules, and one draw needn't show every extreme that they name: `pair_clips`: within the 4 pairs of one device (aligned blocks), one clip, the same for every device and drawn from the seed, is named exactly twice, one other clip is not named, and every remaining clip is named exactly once.
All inputs are finite; a program needn't handle non-finite values.
Results may differ from a plain program's by a relative error of at most 0.0049.
Values may be sent and summed in bfloat16 or wider, within the bound.
A program may use at most 64 MiB of HBM per device.

v0:
```python
import jax
import jax.numpy as jnp
from jax import lax
from jax.sharding import PartitionSpec as P

HEAD_DIM = 128


def attend(queries, own_keys, own_values, pre_keys, pre_values):
    score_scale = queries.shape[-1] ** (-0.5)
    s_pre = (
        jnp.einsum("btkgd,lkd->btkgl", queries, pre_keys, preferred_element_type=jnp.float32)
        * score_scale
    )
    s_own = (
        jnp.einsum("btkgd,bjkd->btkgj", queries, own_keys, preferred_element_type=jnp.float32)
        * score_scale
    )
    tokens = queries.shape[1]
    causal = jnp.arange(tokens)[:, None] >= jnp.arange(tokens)[None, :]
    s_own = jnp.where(causal[None, :, None, None, :], s_own, -jnp.inf)
    row_max = jnp.maximum(jnp.max(s_pre, axis=-1), jnp.max(s_own, axis=-1))
    p_pre = jnp.exp(s_pre - row_max[..., None])
    p_own = jnp.exp(s_own - row_max[..., None])
    row_total = jnp.sum(p_pre, axis=-1) + jnp.sum(p_own, axis=-1)
    w_pre = (p_pre / row_total[..., None]).astype(jnp.bfloat16)
    w_own = (p_own / row_total[..., None]).astype(jnp.bfloat16)
    result = jnp.einsum("btkgl,lkd->btkgd", w_pre, pre_values, preferred_element_type=jnp.float32)
    result = result + jnp.einsum(
        "btkgj,bjkd->btkgd", w_own, own_values, preferred_element_type=jnp.float32
    )
    return result.astype(jnp.bfloat16)


def split_rows(block_rows, head_dim):
    width = block_rows.shape[-1] - 2 * head_dim
    queries = block_rows[..., :width]
    queries = queries.reshape(queries.shape[:-1] + (width // head_dim, head_dim))
    own_keys = block_rows[..., width : width + head_dim]
    own_values = block_rows[..., width + head_dim :]
    return (queries, own_keys, own_values)


def pick_block(slots, per_slot):
    block_slots = min(slots, max(1, 1024 // per_slot))
    while slots % block_slots:
        block_slots -= 1
    return block_slots


def serve(received, pre_keys, pre_values, head_dim):
    slot_shape = received.shape
    slots = slot_shape[0] * slot_shape[1]
    tokens = slot_shape[2]
    kv_here = slot_shape[3]
    heads_per = (slot_shape[4] - 2 * head_dim) // head_dim
    block_slots = pick_block(slots, tokens * kv_here * heads_per)
    blocks = received.reshape((slots // block_slots, block_slots) + slot_shape[2:])

    def attend_block(block_rows):
        queries, own_keys, own_values = split_rows(block_rows, head_dim)
        output = attend(queries, own_keys, own_values, pre_keys, pre_values)
        return output.reshape(block_slots, tokens, kv_here, heads_per * head_dim)

    finished = lax.map(attend_block, blocks)
    finished = finished.reshape(slot_shape[:4] + (heads_per * head_dim,))
    return lax.all_to_all(finished, "clip", split_axis=0, concat_axis=0, tiled=True)


def on_device(pair_clips, pair_rows, prefix_kv):
    owner_count = lax.axis_size("clip")
    my_index = lax.axis_index("clip")
    pairs_here = pair_rows.shape[0]
    tokens = pair_rows.shape[1]
    kv_here = pair_rows.shape[2]
    head_dim = HEAD_DIM
    out_width = pair_rows.shape[3] - 2 * head_dim
    clips_here = lax.dynamic_slice_in_dim(pair_clips, my_index * pairs_here, pairs_here)
    pre_keys = prefix_kv[0, :, :, :head_dim]
    pre_values = prefix_kv[0, :, :, head_dim:]
    owners = jnp.arange(owner_count, dtype=jnp.int32)
    names_owner = clips_here[None, :] == owners[:, None]
    same_clip = clips_here[:, None] == clips_here[None, :]
    earlier = jnp.arange(pairs_here)[:, None] > jnp.arange(pairs_here)[None, :]
    slot_rank = jnp.sum(same_clip & earlier, axis=1)
    flat_rows = pair_rows.reshape(pairs_here, -1)
    capacity = 2
    selector_mask = names_owner[:, None, :] & (
        slot_rank[None, None, :] == jnp.arange(capacity)[None, :, None]
    )
    selector_mask = selector_mask.reshape(owner_count * capacity, pairs_here)
    selector = selector_mask.astype(jnp.bfloat16)
    outgoing = jnp.dot(selector, flat_rows, preferred_element_type=jnp.float32).astype(jnp.bfloat16)
    outgoing = outgoing.reshape((owner_count, capacity) + pair_rows.shape[1:])
    returned = serve(
        lax.all_to_all(outgoing, "clip", split_axis=0, concat_axis=0, tiled=True),
        pre_keys=pre_keys,
        pre_values=pre_values,
        head_dim=head_dim,
    )
    returned = returned.reshape(owner_count * capacity, -1)
    gathered = jnp.dot(selector.T, returned, preferred_element_type=jnp.float32)
    return gathered.astype(jnp.bfloat16).reshape(pairs_here, tokens, kv_here, out_width)


def solution(mesh):
    return jax.shard_map(
        on_device,
        mesh=mesh,
        in_specs=(
            P("grp"),
            P(("grp", "clip"), None, "head", None),
            P(("grp", "clip"), None, "head", None),
        ),
        out_specs=P(("grp", "clip"), None, "head", None),
        check_vma=False,
    )
```

profile of v0, /device:TPU:0, one launch (start us, length us, event | category | flops | bytes accessed | tf_op | source)
XLA Modules:
  0.0 121.9 jit_solution(17837616700038278541)
XLA Ops:
  0.0 0.7 dynamic_slice.7
  1.1 1.5 %reshape.99 = bf16[4,81920]{1,0:T(4,128)(2,1)S(1)} reshape(bf16[4,32,2,1280]{3,2,1,0:T(2,128)(2,1)} %param.6) | data formatting | bytes 1310720 | tf_op jit(solution)/shard_map/reshape | solution.py:86
  2.6 0.6 convolution_convert_fusion
  3.2 1.1 reshape.100
  4.3 1.3 %copy.53 = bf16[4,2,32,2,1280]{4,2,3,1,0:T(8,128)(2,1)} copy(bf16[4,2,32,2,1280]{4,3,2,1,0:T(2,128)(2,1)S(1)} %reshape.100) | data formatting | bytes 2621440 | tf_op jit(solution)/shard_map/reshape | solution.py:94
  5.6 6.3 %all-to-all-start = ((bf16[4,2,32,2,1280]{4,2,3,1,0:T(8,128)(2,1)}), bf16[4,2,32,2,1280]{4,2,3,1,0:T(8,128)(2,1)S(1)}, u32[]{:S(2)}, u32[]{:S(2)}) async-start(bf16[4,2,32,2,1280]{4,2,3,1,0:T(8,128)(2,1)} %copy.53), calls=%async_computation | async-start | bytes 2621440 | tf_op jit(solution)/shard_map/all_to_all | solution.py:96
  11.9 0.7 fusion.19
  12.7 0.9 copy_bitcast_fusion
  13.6 29.7 %all-to-all-done = bf16[4,2,32,2,1280]{4,2,3,1,0:T(8,128)(2,1)S(1)} async-done(((bf16[4,2,32,2,1280]{4,2,3,1,0:T(8,128)(2,1)}), bf16[4,2,32,2,1280]{4,2,3,1,0:T(8,128)(2,1)S(1)}, u32[]{:S(2)}, u32[]{:S(2)}) %all-to-all-start) | async-done | bytes 1310752 | tf_op jit(solution)/shard_map/all_to_all | solution.py:96
  43.3 46.2 %while.10 = (s32[]{:T(128)}, bf16[4,2,32,2,1024]{4,2,1,3,0:T(8,128)(2,1)}, bf16[4,2,32,2,1280]{4,2,3,1,0:T(8,128)(2,1)S(1)}, bf16[1024,2,128]{2,0,1:T(8,128)(2,1)S(1)}, bf16[1024,2,128]{2,0,1:T(8,128)(2,1)}, /*index=5*/s32[]{:T(128)}) while((s32[]{:T(128)}, bf16[4,2,32,2,1024]{4,2,1,3,0:T(8,128)(2,1)}, ...), condition=%wide.region_6.7_spmd, body=%wide.region_1.6_spmd.sunk | while | flops 563608576 | bytes 19502664 | solution.py:65
  44.0 2.6 %bitcast_reduce_fusion.2 = (f32[2,32,2,8]{3,1,0,2:T(8,128)S(1)}, f32[2,2,32,8,1024]{4,3,2,1,0:T(8,128)}) fusion(bf16[1024,2,128]{2,0,1:T(8,128)(2,1)S(1)} %get-tuple-element.111, bf16[2,32,2,8,128]{4,3,1,2,0:T(8,128)(2,1)S(1)} %bitcast.109), kind=kOutput, calls=%fused_computation.1.clone.1 | convolution fusion | flops 270531584 | bytes 4984832 | tf_op jit(solution)/shard_map/while/body/eval_jaxpr/btkgd,lkd->btkgl/dot_general | solution.py:12
  46.9 3.1 %fusion.37 = f32[2,32,2,8]{3,1,0,2:T(8,128)S(1)} fusion(f32[2,2,32,8,1024]{4,3,2,1,0:T(8,128)} %get-tuple-element.91, f32[2,32,2,8]{3,1,0,2:T(8,128)S(1)} %copy.97), kind=kLoop, calls=%fused_computation.4.clone.1 | loop fusion | flops 3144704 | bytes 4202496 | tf_op jit(solution)/shard_map/while/body/eval_jaxpr/reduce_sum | solution.py:25
  50.5 3.3 %fusion.39 = f32[2,32,2,8,128]{4,3,1,0,2:T(8,128)S(1)} fusion(f32[2,2,32,8,1024]{4,3,2,1,0:T(8,128)} %get-tuple-element.91, f32[2,32,2,8]{3,1,0,2:T(8,128)S(1)} %copy.99, f32[2,32,2,8]{3,1,0,2:T(8,128)S(1)} %copy.97, bf16[1024,2,128]{2,0,1:T(8,128)(2,1)} %get-tuple-element.112), kind=kOutput, calls=%fused_computation.6.clone.1 | convolution fusion | flops 272629760 | bytes 5251072 | tf_op jit(solution)/shard_map/while/body/eval_jaxpr/btkgl,lkd->btkgd/dot_general | solution.py:28
  54.1 0.7 constant_dynamic-update-slice_fusion.2
  54.9 0.5 fusion.36
  55.5 2.6 %bitcast_reduce_fusion.2 = (f32[2,32,2,8]{3,1,0,2:T(8,128)S(1)}, f32[2,2,32,8,1024]{4,3,2,1,0:T(8,128)}) fusion(bf16[1024,2,128]{2,0,1:T(8,128)(2,1)S(1)} %get-tuple-element.111, bf16[2,32,2,8,128]{4,3,1,2,0:T(8,128)(2,1)S(1)} %bitcast.109), kind=kOutput, calls=%fused_computation.1.clone.1 | convolution fusion | flops 270531584 | bytes 4984832 | tf_op jit(solution)/shard_map/while/body/eval_jaxpr/btkgd,lkd->btkgl/dot_general | solution.py:12
  58.5 3.1 %fusion.37 = f32[2,32,2,8]{3,1,0,2:T(8,128)S(1)} fusion(f32[2,2,32,8,1024]{4,3,2,1,0:T(8,128)} %get-tuple-element.91, f32[2,32,2,8]{3,1,0,2:T(8,128)S(1)} %copy.97), kind=kLoop, calls=%fused_computation.4.clone.1 | loop fusion | flops 3144704 | bytes 4202496 | tf_op jit(solution)/shard_map/while/body/eval_jaxpr/reduce_sum | solution.py:25
  62.0 3.3 %fusion.39 = f32[2,32,2,8,128]{4,3,1,0,2:T(8,128)S(1)} fusion(f32[2,2,32,8,1024]{4,3,2,1,0:T(8,128)} %get-tuple-element.91, f32[2,32,2,8]{3,1,0,2:T(8,128)S(1)} %copy.99, f32[2,32,2,8]{3,1,0,2:T(8,128)S(1)} %copy.97, bf16[1024,2,128]{2,0,1:T(8,128)(2,1)} %get-tuple-element.112), kind=kOutput, calls=%fused_computation.6.clone.1 | convolution fusion | flops 272629760 | bytes 5251072 | tf_op jit(solution)/shard_map/while/body/eval_jaxpr/btkgl,lkd->btkgd/dot_general | solution.py:28
  65.6 0.7 constant_dynamic-update-slice_fusion.2
  66.5 0.5 fusion.36
  67.1 2.6 %bitcast_reduce_fusion.2 = (f32[2,32,2,8]{3,1,0,2:T(8,128)S(1)}, f32[2,2,32,8,1024]{4,3,2,1,0:T(8,128)}) fusion(bf16[1024,2,128]{2,0,1:T(8,128)(2,1)S(1)} %get-tuple-element.111, bf16[2,32,2,8,128]{4,3,1,2,0:T(8,128)(2,1)S(1)} %bitcast.109), kind=kOutput, calls=%fused_computation.1.clone.1 | convolution fusion | flops 270531584 | bytes 4984832 | tf_op jit(solution)/shard_map/while/body/eval_jaxpr/btkgd,lkd->btkgl/dot_general | solution.py:12
  70.0 3.1 %fusion.37 = f32[2,32,2,8]{3,1,0,2:T(8,128)S(1)} fusion(f32[2,2,32,8,1024]{4,3,2,1,0:T(8,128)} %get-tuple-element.91, f32[2,32,2,8]{3,1,0,2:T(8,128)S(1)} %copy.97), kind=kLoop, calls=%fused_computation.4.clone.1 | loop fusion | flops 3144704 | bytes 4202496 | tf_op jit(solution)/shard_map/while/body/eval_jaxpr/reduce_sum | solution.py:25
  73.6 3.3 %fusion.39 = f32[2,32,2,8,128]{4,3,1,0,2:T(8,128)S(1)} fusion(f32[2,2,32,8,1024]{4,3,2,1,0:T(8,128)} %get-tuple-element.91, f32[2,32,2,8]{3,1,0,2:T(8,128)S(1)} %copy.99, f32[2,32,2,8]{3,1,0,2:T(8,128)S(1)} %copy.97, bf16[1024,2,128]{2,0,1:T(8,128)(2,1)} %get-tuple-element.112), kind=kOutput, calls=%fused_computation.6.clone.1 | convolution fusion | flops 272629760 | bytes 5251072 | tf_op jit(solution)/shard_map/while/body/eval_jaxpr/btkgl,lkd->btkgd/dot_general | solution.py:28
  77.2 0.7 constant_dynamic-update-slice_fusion.2
  78.6 2.6 %bitcast_reduce_fusion.2 = (f32[2,32,2,8]{3,1,0,2:T(8,128)S(1)}, f32[2,2,32,8,1024]{4,3,2,1,0:T(8,128)}) fusion(bf16[1024,2,128]{2,0,1:T(8,128)(2,1)S(1)} %get-tuple-element.111, bf16[2,32,2,8,128]{4,3,1,2,0:T(8,128)(2,1)S(1)} %bitcast.109), kind=kOutput, calls=%fused_computation.1.clone.1 | convolution fusion | flops 270531584 | bytes 4984832 | tf_op jit(solution)/shard_map/while/body/eval_jaxpr/btkgd,lkd->btkgl/dot_general | solution.py:12
  81.6 3.1 %fusion.37 = f32[2,32,2,8]{3,1,0,2:T(8,128)S(1)} fusion(f32[2,2,32,8,1024]{4,3,2,1,0:T(8,128)} %get-tuple-element.91, f32[2,32,2,8]{3,1,0,2:T(8,128)S(1)} %copy.97), kind=kLoop, calls=%fused_computation.4.clone.1 | loop fusion | flops 3144704 | bytes 4202496 | tf_op jit(solution)/shard_map/while/body/eval_jaxpr/reduce_sum | solution.py:25
  85.1 3.3 %fusion.39 = f32[2,32,2,8,128]{4,3,1,0,2:T(8,128)S(1)} fusion(f32[2,2,32,8,1024]{4,3,2,1,0:T(8,128)} %get-tuple-element.91, f32[2,32,2,8]{3,1,0,2:T(8,128)S(1)} %copy.99, f32[2,32,2,8]{3,1,0,2:T(8,128)S(1)} %copy.97, bf16[1024,2,128]{2,0,1:T(8,128)(2,1)} %get-tuple-element.112), kind=kOutput, calls=%fused_computation.6.clone.1 | convolution fusion | flops 272629760 | bytes 5251072 | tf_op jit(solution)/shard_map/while/body/eval_jaxpr/btkgl,lkd->btkgd/dot_general | solution.py:28
  88.8 0.7 constant_dynamic-update-slice_fusion.2
  89.5 28.7 %all_to_all.10 = bf16[4,2,32,2,1024]{4,2,1,3,0:T(8,128)(2,1)S(1)} all-to-all(bf16[4,2,32,2,1024]{4,2,1,3,0:T(8,128)(2,1)} %get-tuple-element.32), channel_id=1, replica_groups=mesh['grp'=2,'clip'=4,'head'=4] {'clip'}, dimensions={0} | all-to-all | bytes 2097152 | tf_op jit(solution)/shard_map/all_to_all | solution.py:67
  118.2 1.1 copy.56
  119.3 0.8 reshape.101
  120.5 1.3 %reshape.102 = bf16[4,32,2,1024]{3,2,1,0:T(2,128)(2,1)} reshape(bf16[4,65536]{1,0:T(4,128)(2,1)S(1)} %convolution_convert_fusion.1) | data formatting | bytes 1048576 | tf_op jit(solution)/shard_map/reshape | solution.py:103
  (71 shorter events, 6.8 us)
Async XLA Ops:
  4.3 7.6 %copy-start = (bf16[1,1024,2,256]{3,2,1,0:T(2,128)(2,1)S(1)}, bf16[1,1024,2,256]{3,2,1,0:T(2,128)(2,1)}, u32[]{:S(2)}) copy-start(bf16[1,1024,2,256]{3,2,1,0:T(2,128)(2,1)} %param.7) | copy-start | bytes 3145732
  5.6 37.7 %all-to-all-start = ((bf16[4,2,32,2,1280]{4,2,3,1,0:T(8,128)(2,1)}), bf16[4,2,32,2,1280]{4,2,3,1,0:T(8,128)(2,1)S(1)}, u32[]{:S(2)}, u32[]{:S(2)}) async-start(bf16[4,2,32,2,1280]{4,2,3,1,0:T(8,128)(2,1)} %copy.53), calls=%async_computation | async-start | bytes 2621440 | tf_op jit(solution)/shard_map/all_to_all | solution.py:96
where the time goes:
time: 122 us
  waiting for transfers between devices  29.7 us (24%)
  blocking collectives  28.7 us (24%)
  matrix products  27.6 us (23%)
  local copies, waits for them, and re-layouts  15.5 us (13%)
  other arithmetic  13.6 us (11%)
  starting transfers between devices  6.32 us (5%)
    all_to_all x1, waiting for transfers between devices, on_device(): lax.all_to_all(outgoing, 'clip', split_axis=0, concat_axis=0, tiled=True)  29.7 us
    all_to_all x1, blocking collectives, serve(): lax.all_to_all(finished, 'clip', split_axis=0, concat_axis=0, tiled=True)  28.7 us
    dot_general x4, matrix products, attend(): jnp.einsum('btkgl,lkd->btkgd', w_pre, pre_values, preferred_element_type=...  13.1 us
    reduce_sum x8, other arithmetic, attend(): row_total = jnp.sum(p_pre, axis=-1) + jnp.sum(p_own, axis=-1)  12.8 us
    dot_general x4, matrix products, attend(): jnp.einsum('btkgd,lkd->btkgl', queries, pre_keys, preferred_element_type=...  10.6 us
    all_to_all x1, starting transfers between devices, on_device(): lax.all_to_all(outgoing, 'clip', split_axis=0, concat_axis=0, tiled=True)  6.32 us
    dynamic_update_slice x4, local copies, waits for them, and re-layouts, serve(): finished = lax.map(attend_block, blocks)  2.91 us
  transfers between devices with their start and end apart: 1, of which 1 were waited for; matrix products, arithmetic and copies ran while one was open for 1% of the time, Pallas kernels for 0%

commit v1 on v0

v1 whole, which is shorter than its diff:
```python
import functools
import math

import jax
import jax.numpy as jnp
from jax import lax
from jax.experimental import pallas as pl
from jax.experimental.pallas import tpu as pltpu
from jax.sharding import PartitionSpec as P

HEAD_DIM = 128
MESH = pl.DeviceIdType.MESH
NT = (((1,), (1,)), ((), ()))


def kernel(n, kv, group, clips_ref, rows_ref, pre_ref, out_ref,
           q_out, q_in, r_out, r_in, s_out, s_in, own_o, own_l, v_ext,
           qs_sem, qr_sem, rs_sem, rr_sem, ss_sem, sr_sem):
    me = lax.axis_index("clip")
    pairs, tokens, _ = rows_ref.shape
    dim = HEAD_DIM
    width = group * dim
    row_w = width + 2 * dim
    prefix = pre_ref.shape[0]
    scale = math.log2(math.e) / math.sqrt(dim)
    tiles = tokens // 8

    def q_copy(peer, r, slot):
        return pltpu.make_async_remote_copy(
            src_ref=q_out.at[peer, r], dst_ref=q_in.at[slot, r],
            send_sem=qs_sem.at[peer, r], recv_sem=qr_sem.at[slot, r],
            device_id={"clip": peer}, device_id_type=MESH)

    def r_copy(peer, r, slot):
        return pltpu.make_async_remote_copy(
            src_ref=r_out.at[peer, r], dst_ref=r_in.at[slot, r],
            send_sem=rs_sem.at[peer, r], recv_sem=rr_sem.at[slot, r],
            device_id={"clip": peer}, device_id_type=MESH)

    def s_copy(peer, r, slot):
        return pltpu.make_async_remote_copy(
            src_ref=s_out.at[peer, r], dst_ref=s_in.at[slot, r],
            send_sem=ss_sem.at[peer, r], recv_sem=sr_sem.at[slot, r],
            device_id={"clip": peer}, device_id_type=MESH)

    barrier = pltpu.get_barrier_semaphore()

    def greet(t, c):
        pl.semaphore_signal(barrier, inc=1, device_id={"clip": lax.rem(me + t, n)}, device_id_type=MESH)
        return c

    lax.fori_loop(1, n, greet, 0)

    base = me * pairs
    clips = [clips_ref[base + j] for j in range(pairs)]

    def pick(clip):
        first = jnp.int32(0)
        last = jnp.int32(0)
        for j in range(pairs):
            last = jnp.where(clips[j] == clip, j, last)
            first = jnp.where(clips[pairs - 1 - j] == clip, pairs - 1 - j, first)
        return first, last

    def pack(dst, peer):
        for r, pair in enumerate(pick(peer)):
            for k in range(kv):
                dst[peer, r, :, k * width:(k + 1) * width] = rows_ref[pair, :, k * row_w:k * row_w + width]

    def pack_peer(t, c):
        pack(q_out, lax.rem(me + t, n))
        return c

    lax.fori_loop(1, n, pack_peer, 0)
    pl.semaphore_wait(barrier, n - 1)

    def send_peer(t, c):
        peer = lax.rem(me + t, n)
        for r in range(2):
            q_copy(peer, r, me).start()
        return c

    lax.fori_loop(1, n, send_peer, 0)
    pack(q_in, me)

    for k in range(kv):
        v_ext[k, :, :dim] = pre_ref[:, k * 2 * dim + dim:(k + 1) * 2 * dim]
        v_ext[k, :, dim:] = jnp.ones((prefix, dim), jnp.bfloat16)

    def queries(ref, *at, start):
        return jnp.concatenate(
            [ref[(*at, slice(None), slice(start + g * dim, start + (g + 1) * dim))] for g in range(group)], axis=0)

    rows_of = group * tokens
    token = lax.rem(lax.broadcasted_iota(jnp.int32, (rows_of, tokens), 0), tokens)
    causal = token >= lax.broadcasted_iota(jnp.int32, (rows_of, tokens), 1)

    def attend_own(j, c):
        for k in range(kv):
            q = queries(rows_ref, j, start=k * row_w)
            keys = rows_ref[j, :, k * row_w + width:k * row_w + width + dim]
            values = rows_ref[j, :, k * row_w + width + dim:(k + 1) * row_w]
            s = lax.dot_general(q, keys, NT, preferred_element_type=jnp.float32)
            s = jnp.where(causal, s, -jnp.inf)
            top = jnp.max(s, axis=1, keepdims=True)
            p = jnp.exp2((s - top) * scale)
            total = jnp.broadcast_to(jnp.sum(p, axis=1, keepdims=True), (rows_of, dim))
            o = jnp.dot(p.astype(jnp.bfloat16), values, preferred_element_type=jnp.float32)
            own_o[j, k] = o / total
            own_l[j, k] = jnp.log2(total) + top * scale
        return c

    lax.fori_loop(0, pairs, attend_own, 0)

    lane = lax.broadcasted_iota(jnp.int32, (8, 128), 1)

    def serve(t, c):
        src = lax.rem(me - t + n, n)
        for r in range(2):
            @pl.when(t > 0)
            def _():
                q_copy(src, r, src).wait_recv()

            stats = jnp.zeros((8, 128), jnp.float32)
            for k in range(kv):
                q = queries(q_in, src, r, start=k * width)
                keys = pre_ref[:, k * 2 * dim:k * 2 * dim + dim]
                s = lax.dot_general(q, keys, NT, preferred_element_type=jnp.float32)
                top = jnp.max(s, axis=1, keepdims=True)
                p = jnp.exp2((s - top) * scale).astype(jnp.bfloat16)
                o = jnp.dot(p, v_ext[k], preferred_element_type=jnp.float32)
                total = o[:, dim:]
                o = (o[:, :dim] / total).astype(jnp.bfloat16)
                level = jnp.log2(total) + top * scale
                for g in range(group):
                    r_out[src, r, :, (k * group + g) * dim:(k * group + g + 1) * dim] = o[g * tokens:(g + 1) * tokens]
                    for i in range(tiles):
                        at = g * tokens + i * 8
                        stats = jnp.where(lane == i * kv * group + k * group + g, level[at:at + 8], stats)
            s_out[src, r] = stats

            @pl.when(t > 0)
            def _():
                s_copy(src, r, me).start()
                r_copy(src, r, me).start()
        return c

    lax.fori_loop(0, n, serve, 0)
    r_in[me] = r_out[me]
    s_in[me] = s_out[me]

    def finish(t, c):
        peer = lax.rem(me + t, n)
        for r in range(2):
            q_copy(peer, r, me).wait_send()
            r_copy(peer, r, peer).wait()
            s_copy(peer, r, peer).wait()
        return c

    lax.fori_loop(1, n, finish, 0)

    for j in range(pairs):
        rank = jnp.int32(0)
        for i in range(j):
            rank = jnp.where(clips[i] == clips[j], 1, rank)
        stats = s_in[clips[j], rank]
        for k in range(kv):
            for g in range(group):
                cols = slice((k * group + g) * dim, (k * group + g + 1) * dim)
                got = r_in[clips[j], rank, :, cols].astype(jnp.float32)
                level = jnp.concatenate(
                    [jnp.broadcast_to(stats[:, c:c + 1], (8, dim))
                     for c in (i * kv * group + k * group + g for i in range(tiles))], axis=0)
                rows = slice(g * tokens, (g + 1) * tokens)
                w_pre = 1.0 / (1.0 + jnp.exp2(own_l[j, k, rows] - level))
                mine = own_o[j, k, rows]
                out_ref[j, :, cols] = (mine + w_pre * (got - mine)).astype(jnp.bfloat16)


def on_device(n, pair_clips, pair_rows, prefix_kv):
    pairs, tokens, kv, row_w = pair_rows.shape
    group = row_w // HEAD_DIM - 2
    width = group * HEAD_DIM
    prefix = prefix_kv.shape[1]
    slots = (n, 2, tokens, kv * width)
    stats = (n, 2, 8, 128)
    own = (pairs, kv, group * tokens, HEAD_DIM)
    flops = 4 * n * 2 * kv * group * tokens * prefix * HEAD_DIM
    out = pl.pallas_call(
        functools.partial(kernel, n, kv, group),
        out_shape=jax.ShapeDtypeStruct((pairs, tokens, kv * width), jnp.bfloat16),
        in_specs=[pl.BlockSpec(memory_space=pltpu.SMEM)] + [pl.BlockSpec(memory_space=pltpu.VMEM)] * 2,
        out_specs=pl.BlockSpec(memory_space=pltpu.VMEM),
        scratch_shapes=[pltpu.VMEM(slots, jnp.bfloat16)] * 4 + [pltpu.VMEM(stats, jnp.float32)] * 2
        + [pltpu.VMEM(own, jnp.float32)] * 2
        + [pltpu.VMEM((kv, prefix, 2 * HEAD_DIM), jnp.bfloat16)]
        + [pltpu.SemaphoreType.DMA((n, 2))] * 6,
        compiler_params=pltpu.CompilerParams(
            collective_id=0, has_side_effects=True, vmem_limit_bytes=48 * 1024 * 1024),
        cost_estimate=pl.CostEstimate(
            flops=flops, bytes_accessed=4 * 1024 * 1024, transcendentals=0),
    )(pair_clips, pair_rows.reshape(pairs, tokens, kv * row_w), prefix_kv.reshape(prefix, kv * 2 * HEAD_DIM))
    return out.reshape(pairs, tokens, kv, width)


def solution(mesh):
    return jax.shard_map(
        functools.partial(on_device, mesh.shape["clip"]),
        mesh=mesh,
        in_specs=(
            P("grp"),
            P(("grp", "clip"), None, "head", None),
            P(("grp", "clip"), None, "head", None),
        ),
        out_specs=P(("grp", "clip"), None, "head", None),
        check_vma=False,
    )
```

time: 122 us -> 60.9 us (0.50)
  Pallas kernels: 0 us -> 56.3 us
  waiting for transfers between devices: 29.7 us -> 0 us
  blocking collectives: 28.7 us -> 0 us
  matrix products: 27.6 us -> 0 us
  other arithmetic: 13.6 us -> 0 us
  local copies, waits for them, and re-layouts: 15.5 us -> 4.36 us
  starting transfers between devices: 6.32 us -> 0 us
    pallas_call x0 -> x1, Pallas kernels: none -> 56.3 us  [on_device(): pl.pallas_call(functools.partial(kernel, n, kv, group), out_shape=jax.Sha...]
    all_to_all x1 -> x0, waiting for transfers between devices: 29.7 us -> none  [on_device(): lax.all_to_all(outgoing, 'clip', split_axis=0, concat_axis=0, tiled=True)]
    all_to_all x1 -> x0, blocking collectives: 28.7 us -> none  [serve(): lax.all_to_all(finished, 'clip', split_axis=0, concat_axis=0, tiled=True)]
    dot_general x18 -> x0, matrix products: 27.6 us -> none  [the longest x4 13.1 us: attend(): jnp.einsum('btkgl,lkd->btkgd', w_pre, pre_values, preferred_element_type=...]
    reduce_sum x9 -> x0, other arithmetic: 12.9 us -> none  [the longest x8 12.8 us: attend(): row_total = jnp.sum(p_pre, axis=-1) + jnp.sum(p_own, axis=-1)]
    all_to_all x1 -> x0, starting transfers between devices: 6.32 us -> none  [on_device(): lax.all_to_all(outgoing, 'clip', split_axis=0, concat_axis=0, tiled=True)]
    dynamic_update_slice x4 -> x0, local copies, waits for them, and re-layouts: 2.91 us -> none  [serve(): finished = lax.map(attend_block, blocks)]
    reshape x5 -> x2, local copies, waits for them, and re-layouts: 5.99 us -> 3.48 us  [the longest x1 2.31 us: on_device(): pair_rows.reshape(pairs, tokens, kv * row_w)]
  transfers between devices with their start and end apart: 1 -> 0, of which waited for: 1 -> 0; matrix products, arithmetic and copies ran while one was open for 1% -> 0% of each run, Pallas kernels for 0% -> 0%
where the time goes in v1:
time: 60.9 us; the launch traced here: 60.7 us
  Pallas kernels  56.3 us (92%)
  local copies, waits for them, and re-layouts  4.36 us (7%)
    pallas_call x1, Pallas kernels, on_device(): pl.pallas_call(functools.partial(kernel, n, kv, group), out_shape=jax.Sha...  56.3 us
    reshape x1, local copies, waits for them, and re-layouts, on_device(): pair_rows.reshape(pairs, tokens, kv * row_w)  2.31 us

profile of v1, /device:TPU:0, one launch (start us, length us, event | category | flops | bytes accessed | tf_op | source)
XLA Modules:
  0.0 60.7 jit_solution(16903893367779745421)
XLA Ops:
  0.0 0.0 copy-start.1
  0.0 2.3 %reshape.9.rows_ref = bf16[4,32,2560]{2,1,0:T(8,128)(2,1)S(1)} reshape(bf16[4,32,2,1280]{3,2,1,0:T(2,128)(2,1)} %param.4) | data formatting | bytes 1310720 | tf_op jit(solution)/shard_map/reshape | solution.py:202
  2.3 0.0 copy-done.1
  2.3 0.2 copy.4
  2.6 0.0 copy-start
  2.6 0.6 %copy-done = s32[16]{0:T(128)S(1)} copy-done((s32[16]{0:T(128)S(1)}, s32[16]{0:T(128)}, u32[]{:S(2)}) %copy-start) | copy-done | bytes 88
  3.2 56.3 %shard_map.37 = bf16[4,32,2048]{2,1,0:T(8,128)(2,1)S(1)} custom-call(s32[16]{0:T(128)S(1)} %copy-done, bf16[4,32,2560]{2,1,0:T(8,128)(2,1)S(1)} %reshape.9.rows_ref, bf16[1024,512]{1,0:T(8,128)(2,1)S(1)} %bitcast.3), custom_call_target="tpu_custom_call" | custom-call | flops 2147483648 | bytes 4194304 | tf_op jit(solution)/shard_map/pallas_call | solution.py:189
  59.6 1.2 %reshape.11 = bf16[4,32,2,1024]{3,2,1,0:T(2,128)(2,1)} reshape(bf16[4,32,2048]{2,1,0:T(8,128)(2,1)S(1)} %shard_map.37) | data formatting | bytes 1048576 | tf_op jit(solution)/shard_map/reshape | solution.py:203
Async XLA Ops:
  0.0 2.3 %copy-start.1 = (bf16[1,1024,2,256]{3,2,1,0:T(2,128)(2,1)S(1)}, bf16[1,1024,2,256]{3,2,1,0:T(2,128)(2,1)}, u32[]{:S(2)}) copy-start(bf16[1,1024,2,256]{3,2,1,0:T(2,128)(2,1)} %param.5) | copy-start | bytes 3145732
  2.6 0.7 %copy-start = (s32[16]{0:T(128)S(1)}, s32[16]{0:T(128)}, u32[]{:S(2)}) copy-start(s32[16]{0:T(128)} %clips_ref.1) | copy-start | bytes 196

commit v2 on v1

v2 whole, which is shorter than its diff:
```python
import functools
import math

import jax
import jax.numpy as jnp
from jax import lax
from jax.experimental import pallas as pl
from jax.experimental.pallas import tpu as pltpu
from jax.sharding import PartitionSpec as P

HEAD_DIM = 128
STAT_ROWS = 16
MESH = pl.DeviceIdType.MESH
NT = (((1,), (1,)), ((), ()))


def kernel(n, kv, group, clips_ref, rows_ref, pre_ref, out_ref,
           extra, q_out, q_in, r_out, r_in, e_out, e_in, own_o, own_l, v_ext,
           xs_sem, xr_sem, qs_sem, qr_sem, rs_sem, rr_sem, es_sem, er_sem):
    me = lax.axis_index("clip")
    pairs, tokens, _ = rows_ref.shape
    dim = HEAD_DIM
    width = group * dim
    row_w = width + 2 * dim
    prefix = pre_ref.shape[0]
    scale = math.log2(math.e) / math.sqrt(dim)
    rows_of = group * tokens
    tiles = rows_of // 8
    assert 3 * tiles <= 128

    def x_copy(to, src, side, k):
        return pltpu.make_async_remote_copy(
            src_ref=extra.at[src, k], dst_ref=extra.at[src, k],
            send_sem=xs_sem.at[side, src, k], recv_sem=xr_sem.at[src, k],
            device_id={"clip": to}, device_id_type=MESH)

    def q_copy(peer, slot, k):
        return pltpu.make_async_remote_copy(
            src_ref=q_out.at[peer, k], dst_ref=q_in.at[slot, k],
            send_sem=qs_sem.at[peer, k], recv_sem=qr_sem.at[slot, k],
            device_id={"clip": peer}, device_id_type=MESH)

    def r_copy(peer, slot, k):
        return pltpu.make_async_remote_copy(
            src_ref=r_out.at[peer, k], dst_ref=r_in.at[slot, k],
            send_sem=rs_sem.at[peer, k], recv_sem=rr_sem.at[slot, k],
            device_id={"clip": peer}, device_id_type=MESH)

    def e_copy(to, dest, side, k):
        return pltpu.make_async_remote_copy(
            src_ref=e_out.at[dest, k], dst_ref=e_in.at[side, dest, k],
            send_sem=es_sem.at[dest, k], recv_sem=er_sem.at[side, dest, k],
            device_id={"clip": to}, device_id_type=MESH)

    def inside(i):
        return jnp.logical_and(i >= 0, i < n)

    barrier = pltpu.get_barrier_semaphore()

    def greet(t, c):
        pl.semaphore_signal(barrier, inc=1, device_id={"clip": lax.rem(me + t, n)}, device_id_type=MESH)
        return c

    lax.fori_loop(1, n, greet, 0)

    base = me * pairs
    clips = [clips_ref[base + j] for j in range(pairs)]
    ranks = []
    hot = jnp.int32(0)
    extra_pair = jnp.int32(0)
    for j in range(pairs):
        again = jnp.int32(0)
        for i in range(j):
            again = jnp.where(clips[i] == clips[j], 1, again)
        ranks.append(again)
        hot = jnp.where(again == 1, clips[j], hot)
        extra_pair = jnp.where(again == 1, j, extra_pair)

    def pack(dst, slot, pair):
        for k in range(kv):
            for g in range(group):
                at = k * row_w + g * dim
                dst[slot, k, g * tokens:(g + 1) * tokens] = rows_ref[pair, :, at:at + dim]

    def pack_first(dst, peer):
        first = jnp.int32(0)
        for j in reversed(range(pairs)):
            first = jnp.where(clips[j] == peer, j, first)
        pack(dst, peer, first)

    def pack_peer(t, c):
        pack_first(q_out, lax.rem(me + t, n))
        return c

    pack(extra, me, extra_pair)
    lax.fori_loop(1, n, pack_peer, 0)
    pl.semaphore_wait(barrier, n - 1)

    def send_extra(side, c):
        to = me + 2 * side - 1

        @pl.when(inside(to))
        def _():
            for k in range(kv):
                x_copy(to, me, side, k).start()
        return c

    def send_first(t, c):
        peer = lax.rem(me + t, n)
        for k in range(kv):
            q_copy(peer, me, k).start()
        return c

    lax.fori_loop(0, 2, send_extra, 0)
    lax.fori_loop(1, n, send_first, 0)
    pack_first(q_in, me)

    for k in range(kv):
        v_ext[k, :, :dim] = pre_ref[:, k * 2 * dim + dim:(k + 1) * 2 * dim]
        v_ext[k, :, dim:] = jnp.ones((prefix, dim), jnp.bfloat16)

    token = lax.rem(lax.broadcasted_iota(jnp.int32, (rows_of, tokens), 0), tokens)
    causal = token >= lax.broadcasted_iota(jnp.int32, (rows_of, tokens), 1)
    lane = lax.broadcasted_iota(jnp.int32, (8, 128), 1)
    lane_tile = lax.rem(lane, tiles)

    def attend_own(j, c):
        for k in range(kv):
            q = jnp.concatenate(
                [rows_ref[j, :, k * row_w + g * dim:k * row_w + (g + 1) * dim] for g in range(group)], axis=0)
            keys = rows_ref[j, :, k * row_w + width:k * row_w + width + dim]
            values = rows_ref[j, :, k * row_w + width + dim:(k + 1) * row_w]
            s = lax.dot_general(q, keys, NT, preferred_element_type=jnp.float32)
            s = jnp.where(causal, s, -jnp.inf)
            top = jnp.max(s, axis=1, keepdims=True)
            p = jnp.exp2((s - top) * scale)
            total = jnp.broadcast_to(jnp.sum(p, axis=1, keepdims=True), (rows_of, dim))
            o = jnp.dot(p.astype(jnp.bfloat16), values, preferred_element_type=jnp.float32)
            own_o[j, k] = o / total
            own_l[j, k] = jnp.log2(total) + top * scale
        return c

    def attend(src_ref, src, dst_ref, k):
        keys = pre_ref[:, k * 2 * dim:k * 2 * dim + dim]
        s = lax.dot_general(src_ref[src, k], keys, NT, preferred_element_type=jnp.float32)
        top = jnp.max(s, axis=1, keepdims=True)
        p = jnp.exp2((s - top) * scale).astype(jnp.bfloat16)
        o = jnp.dot(p, v_ext[k], preferred_element_type=jnp.float32)
        total = o[:, dim:]
        dst_ref[src, k, :rows_of] = (o[:, :dim] / total).astype(jnp.bfloat16)
        level = jnp.log2(total) + top * scale
        stats = jnp.zeros((8, 128), jnp.float32)
        for i in range(tiles):
            stats = jnp.where(lane_tile == i, level[i * 8:(i + 1) * 8], stats)
        high = stats.astype(jnp.bfloat16).astype(jnp.float32)
        middle = (stats - high).astype(jnp.bfloat16).astype(jnp.float32)
        low = stats - high - middle
        parts = jnp.where(lane < tiles, high, jnp.where(lane < 2 * tiles, middle, low))
        dst_ref[src, k, rows_of:] = jnp.concatenate([parts, jnp.zeros_like(parts)], axis=0).astype(jnp.bfloat16)

    def serve_extra(t):
        def one(side, c):
            step = 2 * side - 1
            peer = me + step * t

            @pl.when(inside(peer))
            def _():
                for k in range(kv):
                    x_copy(peer, peer, 1 - side, k).wait_recv()

                    @pl.when(inside(me - step))
                    def _():
                        x_copy(me - step, peer, 1 - side, k).start()

                for k in range(kv):
                    attend(extra, peer, e_out, k)

                    @pl.when(jnp.logical_not(inside(me - step)))
                    def _():
                        e_copy(me + step, peer, side, k).start()
            return c

        lax.fori_loop(0, 2, one, 0)

    def serve_first(t):
        def one(side, c):
            peer = me + (2 * side - 1) * t

            @pl.when(inside(peer))
            def _():
                for k in range(kv):
                    q_copy(peer, peer, k).wait_recv()
                    attend(q_in, peer, r_out, k)
                    r_copy(peer, me, k).start()
            return c

        lax.fori_loop(0, 2, one, 0)

    lax.fori_loop(0, pairs, attend_own, 0)
    for k in range(kv):
        attend(extra, me, e_out, k)
        attend(q_in, me, r_out, k)

    def serve(t, c):
        serve_extra(t)
        serve_first(t)
        return c

    lax.fori_loop(1, n, serve, 0)
    r_in[me] = r_out[me]

    def relay(i, c):
        t = n - 1 - i

        def one(side, d):
            step = 2 * side - 1
            peer = me + step * t

            @pl.when(jnp.logical_and(inside(peer), inside(me - step)))
            def _():
                for k in range(kv):
                    e_copy(me - step, peer, side, k).wait_recv()
                    e_out[peer, k] = jnp.where(hot == me, e_out[peer, k], e_in[side, peer, k])
                    e_copy(me + step, peer, side, k).start()
            return d

        return lax.fori_loop(0, 2, one, c)

    lax.fori_loop(0, n - 1, relay, 0)
    r_in[n] = e_out[me]

    def collect(side, c):
        step = 2 * side - 1

        @pl.when(inside(me - step))
        def _():
            for k in range(kv):
                e_copy(me - step, me, side, k).wait_recv()
                r_in[n, k] = jnp.where((me - hot) * step > 0, e_in[side, me, k], r_in[n, k])
        return c

    lax.fori_loop(0, 2, collect, 0)

    def finish(t, c):
        peer = lax.rem(me + t, n)
        for k in range(kv):
            r_copy(peer, peer, k).wait()
            q_copy(peer, me, k).wait_send()
            e_copy(peer, peer, 0, k).wait_send()
        return c

    lax.fori_loop(1, n, finish, 0)

    def finish_extra(src, c):
        def one(side, d):
            step = 2 * side - 1

            @pl.when(jnp.logical_and((me - src) * step >= 0, inside(me + step)))
            def _():
                for k in range(kv):
                    x_copy(me + step, src, side, k).wait_send()
            return d

        return lax.fori_loop(0, 2, one, c)

    lax.fori_loop(0, n, finish_extra, 0)

    for j in range(pairs):
        slot = jnp.where(ranks[j] == 1, n, clips[j])
        for k in range(kv):
            parts = r_in[slot, k, rows_of:].astype(jnp.float32)[:8]
            stats = parts + pltpu.roll(parts, 128 - tiles, 1) + pltpu.roll(parts, 128 - 2 * tiles, 1)
            for g in range(group):
                rows = slice(g * tokens, (g + 1) * tokens)
                level = jnp.concatenate(
                    [jnp.broadcast_to(stats[:, c:c + 1], (8, dim))
                     for c in range(g * tokens // 8, (g + 1) * tokens // 8)], axis=0)
                w_pre = 1.0 / (1.0 + jnp.exp2(own_l[j, k, rows] - level))
                mine = own_o[j, k, rows]
                got = r_in[slot, k, rows].astype(jnp.float32)
                cols = slice((k * group + g) * dim, (k * group + g + 1) * dim)
                out_ref[j, :, cols] = (mine + w_pre * (got - mine)).astype(jnp.bfloat16)


def on_device(n, pair_clips, pair_rows, prefix_kv):
    pairs, tokens, kv, row_w = pair_rows.shape
    group = row_w // HEAD_DIM - 2
    width = group * HEAD_DIM
    prefix = prefix_kv.shape[1]
    rows_of = group * tokens
    queries = pltpu.VMEM((n, kv, rows_of, HEAD_DIM), jnp.bfloat16)
    result = (kv, rows_of + STAT_ROWS, HEAD_DIM)
    own = pltpu.VMEM((pairs, kv, rows_of, HEAD_DIM), jnp.float32)
    sems = pltpu.SemaphoreType.DMA((n, kv))
    sems_two = pltpu.SemaphoreType.DMA((2, n, kv))
    flops = 4 * n * 2 * kv * rows_of * prefix * HEAD_DIM
    out = pl.pallas_call(
        functools.partial(kernel, n, kv, group),
        out_shape=jax.ShapeDtypeStruct((pairs, tokens, kv * width), jnp.bfloat16),
        in_specs=[pl.BlockSpec(memory_space=pltpu.SMEM)] + [pl.BlockSpec(memory_space=pltpu.VMEM)] * 2,
        out_specs=pl.BlockSpec(memory_space=pltpu.VMEM),
        scratch_shapes=[
            queries, queries, queries,
            pltpu.VMEM((n,) + result, jnp.bfloat16),
            pltpu.VMEM((n + 1,) + result, jnp.bfloat16),
            pltpu.VMEM((n,) + result, jnp.bfloat16),
            pltpu.VMEM((2, n) + result, jnp.bfloat16),
            own, own,
            pltpu.VMEM((kv, prefix, 2 * HEAD_DIM), jnp.bfloat16),
            sems_two, sems, sems, sems, sems, sems, sems, sems_two,
        ],
        compiler_params=pltpu.CompilerParams(
            collective_id=0, has_side_effects=True, vmem_limit_bytes=48 * 1024 * 1024),
        cost_estimate=pl.CostEstimate(
            flops=flops, bytes_accessed=4 * 1024 * 1024, transcendentals=0),
    )(pair_clips, pair_rows.reshape(pairs, tokens, kv * row_w), prefix_kv.reshape(prefix, kv * 2 * HEAD_DIM))
    return out.reshape(pairs, tokens, kv, width)


def solution(mesh):
    return jax.shard_map(
        functools.partial(on_device, mesh.shape["clip"]),
        mesh=mesh,
        in_specs=(
            P("grp"),
            P(("grp", "clip"), None, "head", None),
            P(("grp", "clip"), None, "head", None),
        ),
        out_specs=P(("grp", "clip"), None, "head", None),
        check_vma=False,
    )
```

time: 60.9 us -> 48.6 us (0.80)
  Pallas kernels: 56.3 us -> 44.1 us
    pallas_call x1, Pallas kernels: 56.3 us -> 44.1 us  [on_device(): pl.pallas_call(functools.partial(kernel, n, kv, group), out_shape=jax.Sha...]
where the time goes in v2:
time: 48.6 us; the launch traced here: 48.5 us
  Pallas kernels  44.1 us (91%)
  local copies, waits for them, and re-layouts  4.36 us (9%)
    pallas_call x1, Pallas kernels, on_device(): pl.pallas_call(functools.partial(kernel, n, kv, group), out_shape=jax.Sha...  44.1 us
    reshape x1, local copies, waits for them, and re-layouts, on_device(): pair_rows.reshape(pairs, tokens, kv * row_w)  2.31 us
    reshape x1, local copies, waits for them, and re-layouts, on_device(): return out.reshape(pairs, tokens, kv, width)  1.17 us

profile of v2, /device:TPU:0, one launch (start us, length us, event | category | flops | bytes accessed | tf_op | source)
XLA Modules:
  0.0 48.5 jit_solution(2626708660806822685)
XLA Ops:
  0.0 0.0 copy-start.1
  0.0 2.3 %reshape.9.rows_ref = bf16[4,32,2560]{2,1,0:T(8,128)(2,1)S(1)} reshape(bf16[4,32,2,1280]{3,2,1,0:T(2,128)(2,1)} %param.4) | data formatting | bytes 1310720 | tf_op jit(solution)/shard_map/reshape | solution.py:316
  2.3 0.0 copy-done.1
  2.3 0.2 copy.4
  2.6 0.0 copy-start
  2.6 0.6 %copy-done = s32[16]{0:T(128)S(1)} copy-done((s32[16]{0:T(128)S(1)}, s32[16]{0:T(128)}, u32[]{:S(2)}) %copy-start) | copy-done | bytes 88
  3.2 44.1 %shard_map.37 = bf16[4,32,2048]{2,1,0:T(8,128)(2,1)S(1)} custom-call(s32[16]{0:T(128)S(1)} %copy-done, bf16[4,32,2560]{2,1,0:T(8,128)(2,1)S(1)} %reshape.9.rows_ref, bf16[1024,512]{1,0:T(8,128)(2,1)S(1)} %bitcast.3), custom_call_target="tpu_custom_call" | custom-call | flops 2147483648 | bytes 4194304 | tf_op jit(solution)/shard_map/pallas_call | solution.py:297
  47.3 1.2 %reshape.11 = bf16[4,32,2,1024]{3,2,1,0:T(2,128)(2,1)} reshape(bf16[4,32,2048]{2,1,0:T(8,128)(2,1)S(1)} %shard_map.37) | data formatting | bytes 1048576 | tf_op jit(solution)/shard_map/reshape | solution.py:317
Async XLA Ops:
  0.0 2.3 %copy-start.1 = (bf16[1,1024,2,256]{3,2,1,0:T(2,128)(2,1)S(1)}, bf16[1,1024,2,256]{3,2,1,0:T(2,128)(2,1)}, u32[]{:S(2)}) copy-start(bf16[1,1024,2,256]{3,2,1,0:T(2,128)(2,1)} %param.5) | copy-start | bytes 3145732
  2.6 0.7 %copy-start = (s32[16]{0:T(128)S(1)}, s32[16]{0:T(128)}, u32[]{:S(2)}) copy-start(s32[16]{0:T(128)} %clips_ref.1) | copy-start | bytes 196

commit v3 on v2

v3 whole, which is shorter than its diff:
```python
import functools
import math

import jax
import jax.numpy as jnp
from jax import lax
from jax.experimental import pallas as pl
from jax.experimental.pallas import tpu as pltpu
from jax.sharding import PartitionSpec as P

HEAD_DIM = 128
STAT_ROWS = 16
MESH = pl.DeviceIdType.MESH
NT = (((1,), (1,)), ((), ()))


def kernel(n, kv, group, clips_ref, rows_ref, pre_ref, out_ref,
           extra, q_out, q_in, first, ab_out, ab_in, own_o, own_l, v_ext,
           qs_sem, qr_sem, as_sem, ar_sem):
    me = lax.axis_index("clip")
    pairs, tokens, _ = rows_ref.shape
    dim = HEAD_DIM
    width = group * dim
    row_w = width + 2 * dim
    prefix = pre_ref.shape[0]
    scale = math.log2(math.e) / math.sqrt(dim)
    rows_of = group * tokens
    tiles = rows_of // 8
    assert 3 * tiles <= 128

    def q_copy(peer, slot, k):
        return pltpu.make_async_remote_copy(
            src_ref=q_out.at[peer, k], dst_ref=q_in.at[slot, k],
            send_sem=qs_sem.at[peer, k], recv_sem=qr_sem.at[slot, k],
            device_id={"clip": peer}, device_id_type=MESH)

    def ab_copy(which, peer, slot, k):
        return pltpu.make_async_remote_copy(
            src_ref=ab_out.at[which, peer, k], dst_ref=ab_in.at[which, slot, k],
            send_sem=as_sem.at[which, peer, k], recv_sem=ar_sem.at[which, slot, k],
            device_id={"clip": peer}, device_id_type=MESH)

    def inside(i):
        return jnp.logical_and(i >= 0, i < n)

    barrier = pltpu.get_barrier_semaphore()

    def greet(t, c):
        pl.semaphore_signal(barrier, inc=1, device_id={"clip": lax.rem(me + t, n)}, device_id_type=MESH)
        return c

    lax.fori_loop(1, n, greet, 0)

    base = me * pairs
    clips = [clips_ref[base + j] for j in range(pairs)]
    ranks = []
    hot = jnp.int32(0)
    extra_pair = jnp.int32(0)
    for j in range(pairs):
        again = jnp.int32(0)
        for i in range(j):
            again = jnp.where(clips[i] == clips[j], 1, again)
        ranks.append(again)
        hot = jnp.where(again == 1, clips[j], hot)
        extra_pair = jnp.where(again == 1, j, extra_pair)

    def pack(dst, slot, pair):
        for k in range(kv):
            for g in range(group):
                at = k * row_w + g * dim
                dst[slot, k, g * tokens:(g + 1) * tokens] = rows_ref[pair, :, at:at + dim]

    def pack_first(dst, peer):
        first = jnp.int32(0)
        for j in reversed(range(pairs)):
            first = jnp.where(clips[j] == peer, j, first)
        pack(dst, peer, first)

    def pack_peer(t, c):
        pack_first(q_out, lax.rem(me + t, n))
        return c

    lax.fori_loop(1, n, pack_peer, 0)
    pl.semaphore_wait(barrier, n - 1)

    def peers(body):
        def at(t, c):
            def one(side, d):
                peer = me + (2 * side - 1) * t

                @pl.when(inside(peer))
                def _():
                    body(peer)
                return d

            return lax.fori_loop(0, 2, one, c)

        lax.fori_loop(1, n, at, 0)

    for k in range(kv):
        peers(lambda peer, k=k: q_copy(peer, me, k).start())
    pack_first(q_in, me)
    pack(extra, 0, extra_pair)

    for k in range(kv):
        v_ext[k, :, :dim] = pre_ref[:, k * 2 * dim + dim:(k + 1) * 2 * dim]
        v_ext[k, :, dim:] = jnp.ones((prefix, dim), jnp.bfloat16)

    token = lax.rem(lax.broadcasted_iota(jnp.int32, (rows_of, tokens), 0), tokens)
    causal = token >= lax.broadcasted_iota(jnp.int32, (rows_of, tokens), 1)
    lane = lax.broadcasted_iota(jnp.int32, (8, 128), 1)
    lane_tile = lax.rem(lane, tiles)

    def attend_own(j, c):
        for k in range(kv):
            q = jnp.concatenate(
                [rows_ref[j, :, k * row_w + g * dim:k * row_w + (g + 1) * dim] for g in range(group)], axis=0)
            keys = rows_ref[j, :, k * row_w + width:k * row_w + width + dim]
            values = rows_ref[j, :, k * row_w + width + dim:(k + 1) * row_w]
            s = lax.dot_general(q, keys, NT, preferred_element_type=jnp.float32)
            s = jnp.where(causal, s, -jnp.inf)
            top = jnp.max(s, axis=1, keepdims=True)
            p = jnp.exp2((s - top) * scale)
            total = jnp.broadcast_to(jnp.sum(p, axis=1, keepdims=True), (rows_of, dim))
            o = jnp.dot(p.astype(jnp.bfloat16), values, preferred_element_type=jnp.float32)
            own_o[j, k] = o / total
            own_l[j, k] = jnp.log2(total) + top * scale
        return c

    def attend(q, k, put):
        keys = pre_ref[:, k * 2 * dim:k * 2 * dim + dim]
        s = lax.dot_general(q, keys, NT, preferred_element_type=jnp.float32)
        top = jnp.max(s, axis=1, keepdims=True)
        p = jnp.exp2((s - top) * scale).astype(jnp.bfloat16)
        o = jnp.dot(p, v_ext[k], preferred_element_type=jnp.float32)
        total = o[:, dim:]
        put(slice(0, rows_of), (o[:, :dim] / total).astype(jnp.bfloat16))
        level = jnp.log2(total) + top * scale
        stats = jnp.zeros((8, 128), jnp.float32)
        for i in range(tiles):
            stats = jnp.where(lane_tile == i, level[i * 8:(i + 1) * 8], stats)
        high = stats.astype(jnp.bfloat16).astype(jnp.float32)
        middle = (stats - high).astype(jnp.bfloat16).astype(jnp.float32)
        low = stats - high - middle
        parts = jnp.where(lane < tiles, high, jnp.where(lane < 2 * tiles, middle, low))
        put(slice(rows_of, rows_of + STAT_ROWS),
            jnp.concatenate([parts, jnp.zeros_like(parts)], axis=0).astype(jnp.bfloat16))

    lax.fori_loop(0, pairs, attend_own, 0)
    for k in range(kv):
        def put_first(rows, value, k=k):
            ab_in[0, me, k, rows] = value
            ab_in[1, me, k, rows] = value

        def put_extra(rows, value, k=k):
            ab_in[1, n, k, rows] = value

        attend(q_in[me, k], k, put_first)
        attend(extra[0, k], k, put_extra)

    def serve_first(peer, k):
        q_copy(peer, peer, k).wait_recv()

        def put(rows, value):
            first[peer, k, rows] = value
            if rows.start == 0:
                value = jnp.where(hot == peer, extra[0, k], value)
            ab_out[0, peer, k, rows] = value

        attend(q_in[peer, k], k, put)
        ab_copy(0, peer, me, k).start()

    def serve_extra(peer, k):
        ab_copy(0, peer, peer, k).wait_recv()

        def put(rows, value):
            ab_out[1, peer, k, rows] = jnp.where(hot == peer, first[peer, k, rows], value)

        attend(ab_in[0, peer, k, :rows_of], k, put)
        ab_copy(1, peer, me, k).start()

    for k in range(kv):
        peers(functools.partial(serve_first, k=k))
    for k in range(kv):
        peers(functools.partial(serve_extra, k=k))

    def finish(peer):
        for k in range(kv):
            q_copy(peer, me, k).wait_send()
            ab_copy(0, peer, me, k).wait_send()
            ab_copy(1, peer, peer, k).wait()

    peers(finish)

    for j in range(pairs):
        which = jnp.where(hot == me, 1, ranks[j])
        slot = jnp.where(jnp.logical_and(hot == me, ranks[j] == 1), n, clips[j])
        for k in range(kv):
            parts = ab_in[which, slot, k, rows_of:].astype(jnp.float32)[:8]
            stats = parts + pltpu.roll(parts, 128 - tiles, 1) + pltpu.roll(parts, 128 - 2 * tiles, 1)
            for g in range(group):
                rows = slice(g * tokens, (g + 1) * tokens)
                level = jnp.concatenate(
                    [jnp.broadcast_to(stats[:, c:c + 1], (8, dim))
                     for c in range(g * tokens // 8, (g + 1) * tokens // 8)], axis=0)
                w_pre = 1.0 / (1.0 + jnp.exp2(own_l[j, k, rows] - level))
                mine = own_o[j, k, rows]
                got = ab_in[which, slot, k, rows].astype(jnp.float32)
                cols = slice((k * group + g) * dim, (k * group + g + 1) * dim)
                out_ref[j, :, cols] = (mine + w_pre * (got - mine)).astype(jnp.bfloat16)


def on_device(n, pair_clips, pair_rows, prefix_kv):
    pairs, tokens, kv, row_w = pair_rows.shape
    group = row_w // HEAD_DIM - 2
    width = group * HEAD_DIM
    prefix = prefix_kv.shape[1]
    rows_of = group * tokens
    queries = pltpu.VMEM((n, kv, rows_of, HEAD_DIM), jnp.bfloat16)
    result = (kv, rows_of + STAT_ROWS, HEAD_DIM)
    own = pltpu.VMEM((pairs, kv, rows_of, HEAD_DIM), jnp.float32)
    sems = pltpu.SemaphoreType.DMA((n, kv))
    sems_two = pltpu.SemaphoreType.DMA((2, n, kv))
    flops = 4 * n * 2 * kv * rows_of * prefix * HEAD_DIM
    out = pl.pallas_call(
        functools.partial(kernel, n, kv, group),
        out_shape=jax.ShapeDtypeStruct((pairs, tokens, kv * width), jnp.bfloat16),
        in_specs=[pl.BlockSpec(memory_space=pltpu.SMEM)] + [pl.BlockSpec(memory_space=pltpu.VMEM)] * 2,
        out_specs=pl.BlockSpec(memory_space=pltpu.VMEM),
        scratch_shapes=[
            pltpu.VMEM((1, kv, rows_of, HEAD_DIM), jnp.bfloat16),
            queries, queries,
            pltpu.VMEM((n,) + result, jnp.bfloat16),
            pltpu.VMEM((2, n) + result, jnp.bfloat16),
            pltpu.VMEM((2, n + 1) + result, jnp.bfloat16),
            own, own,
            pltpu.VMEM((kv, prefix, 2 * HEAD_DIM), jnp.bfloat16),
            sems, sems, sems_two, sems_two,
        ],
        compiler_params=pltpu.CompilerParams(
            collective_id=0, has_side_effects=True, vmem_limit_bytes=48 * 1024 * 1024),
        cost_estimate=pl.CostEstimate(
            flops=flops, bytes_accessed=4 * 1024 * 1024, transcendentals=0),
    )(pair_clips, pair_rows.reshape(pairs, tokens, kv * row_w), prefix_kv.reshape(prefix, kv * 2 * HEAD_DIM))
    return out.reshape(pairs, tokens, kv, width)


def solution(mesh):
    return jax.shard_map(
        functools.partial(on_device, mesh.shape["clip"]),
        mesh=mesh,
        in_specs=(
            P("grp"),
            P(("grp", "clip"), None, "head", None),
            P(("grp", "clip"), None, "head", None),
        ),
        out_specs=P(("grp", "clip"), None, "head", None),
        check_vma=False,
    )
```

time: 48.6 us -> 47.6 us (0.979)
  Pallas kernels: 44.1 us -> 43 us
    pallas_call x1, Pallas kernels: 44.1 us -> 43 us  [on_device(): pl.pallas_call(functools.partial(kernel, n, kv, group), out_shape=jax.Sha...]
where the time goes in v3:
time: 47.6 us; the launch traced here: 47.4 us
  Pallas kernels  43 us (90%)
  local copies, waits for them, and re-layouts  4.36 us (9%)
    pallas_call x1, Pallas kernels, on_device(): pl.pallas_call(functools.partial(kernel, n, kv, group), out_shape=jax.Sha...  43 us
    reshape x1, local copies, waits for them, and re-layouts, on_device(): pair_rows.reshape(pairs, tokens, kv * row_w)  2.31 us
    reshape x1, local copies, waits for them, and re-layouts, on_device(): return out.reshape(pairs, tokens, kv, width)  1.17 us

profile of v3, /device:TPU:0, one launch (start us, length us, event | category | flops | bytes accessed | tf_op | source)
XLA Modules:
  0.0 47.4 jit_solution(2315567852062035992)
XLA Ops:
  0.0 0.0 copy-start.1
  0.0 2.3 %reshape.9.rows_ref = bf16[4,32,2560]{2,1,0:T(8,128)(2,1)S(1)} reshape(bf16[4,32,2,1280]{3,2,1,0:T(2,128)(2,1)} %param.4) | data formatting | bytes 1310720 | tf_op jit(solution)/shard_map/reshape | solution.py:244
  2.3 0.0 copy-done.1
  2.3 0.2 copy.4
  2.6 0.0 copy-start
  2.6 0.6 %copy-done = s32[16]{0:T(128)S(1)} copy-done((s32[16]{0:T(128)S(1)}, s32[16]{0:T(128)}, u32[]{:S(2)}) %copy-start) | copy-done | bytes 88
  3.2 43.0 %shard_map.37 = bf16[4,32,2048]{2,1,0:T(8,128)(2,1)S(1)} custom-call(s32[16]{0:T(128)S(1)} %copy-done, bf16[4,32,2560]{2,1,0:T(8,128)(2,1)S(1)} %reshape.9.rows_ref, bf16[1024,512]{1,0:T(8,128)(2,1)S(1)} %bitcast.3), custom_call_target="tpu_custom_call" | custom-call | flops 2147483648 | bytes 4194304 | tf_op jit(solution)/shard_map/pallas_call | solution.py:225
  46.3 1.2 %reshape.11 = bf16[4,32,2,1024]{3,2,1,0:T(2,128)(2,1)} reshape(bf16[4,32,2048]{2,1,0:T(8,128)(2,1)S(1)} %shard_map.37) | data formatting | bytes 1048576 | tf_op jit(solution)/shard_map/reshape | solution.py:245
Async XLA Ops:
  0.0 2.3 %copy-start.1 = (bf16[1,1024,2,256]{3,2,1,0:T(2,128)(2,1)S(1)}, bf16[1,1024,2,256]{3,2,1,0:T(2,128)(2,1)}, u32[]{:S(2)}) copy-start(bf16[1,1024,2,256]{3,2,1,0:T(2,128)(2,1)} %param.5) | copy-start | bytes 3145732
  2.6 0.7 %copy-start = (s32[16]{0:T(128)S(1)}, s32[16]{0:T(128)}, u32[]{:S(2)}) copy-start(s32[16]{0:T(128)} %clips_ref.1) | copy-start | bytes 196

commit v4 on v3

--- a/solution.py
+++ b/solution.py
@@ -15,10 +15,10 @@
 
 
 def kernel(n, kv, group, clips_ref, rows_ref, pre_ref, out_ref,
-           extra, q_out, q_in, first, ab_out, ab_in, own_o, own_l, v_ext,
+           extra, q_out, q_in, first, ab_out, ab_in, own_o, own_l, v_ext, sums,
            qs_sem, qr_sem, as_sem, ar_sem):
     me = lax.axis_index("clip")
-    pairs, tokens, _ = rows_ref.shape
+    pairs, tokens = rows_ref.shape[:2]
     dim = HEAD_DIM
     width = group * dim
     row_w = width + 2 * dim
@@ -26,7 +26,7 @@
     scale = math.log2(math.e) / math.sqrt(dim)
     rows_of = group * tokens
     tiles = rows_of // 8
-    assert 3 * tiles <= 128
+    assert 3 * tiles <= 128 and kv * 8 <= STAT_ROWS
 
     def q_copy(peer, slot, k):
         return pltpu.make_async_remote_copy(
@@ -34,9 +34,13 @@
             send_sem=qs_sem.at[peer, k], recv_sem=qr_sem.at[slot, k],
             device_id={"clip": peer}, device_id_type=MESH)
 
+    def rows_sent(k):
+        return rows_of + (STAT_ROWS if k == kv - 1 else 0)
+
     def ab_copy(which, peer, slot, k):
         return pltpu.make_async_remote_copy(
-            src_ref=ab_out.at[which, peer, k], dst_ref=ab_in.at[which, slot, k],
+            src_ref=ab_out.at[which, peer, k, pl.ds(0, rows_sent(k))],
+            dst_ref=ab_in.at[which, slot, k, pl.ds(0, rows_sent(k))],
             send_sem=as_sem.at[which, peer, k], recv_sem=ar_sem.at[which, slot, k],
             device_id={"clip": peer}, device_id_type=MESH)
 
@@ -64,24 +68,15 @@
         hot = jnp.where(again == 1, clips[j], hot)
         extra_pair = jnp.where(again == 1, j, extra_pair)
 
-    def pack(dst, slot, pair):
-        for k in range(kv):
-            for g in range(group):
-                at = k * row_w + g * dim
-                dst[slot, k, g * tokens:(g + 1) * tokens] = rows_ref[pair, :, at:at + dim]
-
-    def pack_first(dst, peer):
-        first = jnp.int32(0)
+    def pack(dst, slot, pair, k):
+        for g in range(group):
+            dst[slot, k, g * tokens:(g + 1) * tokens] = rows_ref[pair, :, k, g * dim:(g + 1) * dim]
+
+    def pack_first(dst, peer, k):
+        pair = jnp.int32(0)
         for j in reversed(range(pairs)):
-            first = jnp.where(clips[j] == peer, j, first)
-        pack(dst, peer, first)
-
-    def pack_peer(t, c):
-        pack_first(q_out, lax.rem(me + t, n))
-        return c
-
-    lax.fori_loop(1, n, pack_peer, 0)
-    pl.semaphore_wait(barrier, n - 1)
+            pair = jnp.where(clips[j] == peer, j, pair)
+        pack(dst, peer, pair, k)
 
     def peers(body):
         def at(t, c):
@@ -98,9 +93,13 @@
         lax.fori_loop(1, n, at, 0)
 
     for k in range(kv):
+        peers(functools.partial(pack_first, q_out, k=k))
+        if k == 0:
+            pl.semaphore_wait(barrier, n - 1)
         peers(lambda peer, k=k: q_copy(peer, me, k).start())
-    pack_first(q_in, me)
-    pack(extra, 0, extra_pair)
+    for k in range(kv):
+        pack_first(q_in, me, k)
+        pack(extra, 0, extra_pair, k)
 
     for k in range(kv):
         v_ext[k, :, :dim] = pre_ref[:, k * 2 * dim + dim:(k + 1) * 2 * dim]
@@ -114,9 +113,9 @@
     def attend_own(j, c):
         for k in range(kv):
             q = jnp.concatenate(
-                [rows_ref[j, :, k * row_w + g * dim:k * row_w + (g + 1) * dim] for g in range(group)], axis=0)
-            keys = rows_ref[j, :, k * row_w + width:k * row_w + width + dim]
-            values = rows_ref[j, :, k * row_w + width + dim:(k + 1) * row_w]
+                [rows_ref[j, :, k, g * dim:(g + 1) * dim] for g in range(group)], axis=0)
+            keys = rows_ref[j, :, k, width:width + dim]
+            values = rows_ref[j, :, k, width + dim:]
             s = lax.dot_general(q, keys, NT, preferred_element_type=jnp.float32)
             s = jnp.where(causal, s, -jnp.inf)
             top = jnp.max(s, axis=1, keepdims=True)
@@ -127,7 +126,7 @@
             own_l[j, k] = jnp.log2(total) + top * scale
         return c
 
-    def attend(q, k, put):
+    def attend(q, k, at, put):
         keys = pre_ref[:, k * 2 * dim:k * 2 * dim + dim]
         s = lax.dot_general(q, keys, NT, preferred_element_type=jnp.float32)
         top = jnp.max(s, axis=1, keepdims=True)
@@ -143,8 +142,12 @@
         middle = (stats - high).astype(jnp.bfloat16).astype(jnp.float32)
         low = stats - high - middle
         parts = jnp.where(lane < tiles, high, jnp.where(lane < 2 * tiles, middle, low))
-        put(slice(rows_of, rows_of + STAT_ROWS),
-            jnp.concatenate([parts, jnp.zeros_like(parts)], axis=0).astype(jnp.bfloat16))
+        if k < kv - 1:
+            sums[(*at, k)] = parts
+        else:
+            block = [sums[(*at, i)] for i in range(k)] + [parts]
+            block += [jnp.zeros_like(parts)] * (STAT_ROWS // 8 - kv)
+            put(slice(rows_of, rows_of + STAT_ROWS), jnp.concatenate(block, axis=0).astype(jnp.bfloat16))
 
     lax.fori_loop(0, pairs, attend_own, 0)
     for k in range(kv):
@@ -155,8 +158,8 @@
         def put_extra(rows, value, k=k):
             ab_in[1, n, k, rows] = value
 
-        attend(q_in[me, k], k, put_first)
-        attend(extra[0, k], k, put_extra)
+        attend(q_in[me, k], k, (0, me), put_first)
+        attend(extra[0, k], k, (1, me), put_extra)
 
     def serve_first(peer, k):
         q_copy(peer, peer, k).wait_recv()
@@ -167,7 +170,7 @@
                 value = jnp.where(hot == peer, extra[0, k], value)
             ab_out[0, peer, k, rows] = value
 
-        attend(q_in[peer, k], k, put)
+        attend(q_in[peer, k], k, (0, peer), put)
         ab_copy(0, peer, me, k).start()
 
     def serve_extra(peer, k):
@@ -176,7 +179,7 @@
         def put(rows, value):
             ab_out[1, peer, k, rows] = jnp.where(hot == peer, first[peer, k, rows], value)
 
-        attend(ab_in[0, peer, k, :rows_of], k, put)
+        attend(ab_in[0, peer, k, :rows_of], k, (1, peer), put)
         ab_copy(1, peer, me, k).start()
 
     for k in range(kv):
@@ -196,7 +199,7 @@
         which = jnp.where(hot == me, 1, ranks[j])
         slot = jnp.where(jnp.logical_and(hot == me, ranks[j] == 1), n, clips[j])
         for k in range(kv):
-            parts = ab_in[which, slot, k, rows_of:].astype(jnp.float32)[:8]
+            parts = ab_in[which, slot, kv - 1, rows_of:].astype(jnp.float32)[k * 8:(k + 1) * 8]
             stats = parts + pltpu.roll(parts, 128 - tiles, 1) + pltpu.roll(parts, 128 - 2 * tiles, 1)
             for g in range(group):
                 rows = slice(g * tokens, (g + 1) * tokens)
@@ -235,13 +238,14 @@
             pltpu.VMEM((2, n + 1) + result, jnp.bfloat16),
             own, own,
             pltpu.VMEM((kv, prefix, 2 * HEAD_DIM), jnp.bfloat16),
+            pltpu.VMEM((2, n, kv, 8, 128), jnp.float32),
             sems, sems, sems_two, sems_two,
         ],
         compiler_params=pltpu.CompilerParams(
             collective_id=0, has_side_effects=True, vmem_limit_bytes=48 * 1024 * 1024),
         cost_estimate=pl.CostEstimate(
             flops=flops, bytes_accessed=4 * 1024 * 1024, transcendentals=0),
-    )(pair_clips, pair_rows.reshape(pairs, tokens, kv * row_w), prefix_kv.reshape(prefix, kv * 2 * HEAD_DIM))
+    )(pair_clips, pair_rows, prefix_kv.reshape(prefix, kv * 2 * HEAD_DIM))
     return out.reshape(pairs, tokens, kv, width)
 
 

time: 47.6 us -> 46 us (0.966)
  local copies, waits for them, and re-layouts: 4.36 us -> 3.33 us
  Pallas kernels: 43 us -> 42.5 us
    reshape x1 -> x0, local copies, waits for them, and re-layouts: 2.31 us -> none  [on_device(): pair_rows.reshape(pairs, tokens, kv * row_w)]
    unnamed x5, local copies, waits for them, and re-layouts: 0.88 us -> 2.16 us
    pallas_call x1, Pallas kernels: 43 us -> 42.5 us  [on_device(): pl.pallas_call(functools.partial(kernel, n, kv, group), out_shape=jax.Sha...]
where the time goes in v4:
time: 46 us; the launch traced here: 45.9 us
  Pallas kernels  42.5 us (92%)
  local copies, waits for them, and re-layouts  3.33 us (7%)
    pallas_call x1, Pallas kernels, on_device(): pl.pallas_call(functools.partial(kernel, n, kv, group), out_shape=jax.Sha...  42.5 us
    unnamed x5, local copies, waits for them, and re-layouts  2.16 us
    reshape x1, local copies, waits for them, and re-layouts, on_device(): return out.reshape(pairs, tokens, kv, width)  1.17 us

profile of v4, /device:TPU:0, one launch (start us, length us, event | category | flops | bytes accessed | tf_op | source)
XLA Modules:
  0.0 45.9 jit_solution(3213387084159968403)
XLA Ops:
  0.0 0.0 copy-start
  0.0 1.5 %copy.4 = bf16[128,8,2,256]{3,1,2,0:T(8,128)(2,1)S(1)} copy(bf16[128,8,2,256]{3,2,1,0:T(2,128)(2,1)} %bitcast.4) | data formatting | bytes 2097152
  1.5 0.0 copy-start.1
  1.5 0.0 copy-done
  1.5 0.6 %copy-done.1 = s32[16]{0:T(128)S(1)} copy-done((s32[16]{0:T(128)S(1)}, s32[16]{0:T(128)}, u32[]{:S(2)}) %copy-start.1) | copy-done | bytes 88
  2.2 42.5 %shard_map.37 = bf16[4,32,2048]{2,1,0:T(8,128)(2,1)S(1)} custom-call(s32[16]{0:T(128)S(1)} %copy-done.1, bf16[4,32,2,1280]{3,2,1,0:T(2,128)(2,1)S(1)} %copy-done, bf16[1024,512]{1,0:T(8,128)(2,1)S(1)} %bitcast.3), custom_call_target="tpu_custom_call" | custom-call | flops 2147483648 | bytes 4194304 | tf_op jit(solution)/shard_map/pallas_call | solution.py:228
  44.7 1.2 %reshape.7 = bf16[4,32,2,1024]{3,2,1,0:T(2,128)(2,1)} reshape(bf16[4,32,2048]{2,1,0:T(8,128)(2,1)S(1)} %shard_map.37) | data formatting | bytes 1048576 | tf_op jit(solution)/shard_map/reshape | solution.py:249
Async XLA Ops:
  0.0 1.5 %copy-start = (bf16[4,32,2,1280]{3,2,1,0:T(2,128)(2,1)S(1)}, bf16[4,32,2,1280]{3,2,1,0:T(2,128)(2,1)}, u32[]{:S(2)}) copy-start(bf16[4,32,2,1280]{3,2,1,0:T(2,128)(2,1)} %rows_ref.1) | copy-start | bytes 1966084
  1.5 0.7 %copy-start.1 = (s32[16]{0:T(128)S(1)}, s32[16]{0:T(128)}, u32[]{:S(2)}) copy-start(s32[16]{0:T(128)} %clips_ref.1) | copy-start | bytes 196

commit v5 on v4

--- a/solution.py
+++ b/solution.py
@@ -182,10 +182,8 @@
         attend(ab_in[0, peer, k, :rows_of], k, (1, peer), put)
         ab_copy(1, peer, me, k).start()
 
-    for k in range(kv):
-        peers(functools.partial(serve_first, k=k))
-    for k in range(kv):
-        peers(functools.partial(serve_extra, k=k))
+    peers(lambda peer: [serve_first(peer, k) for k in range(kv)])
+    peers(lambda peer: [serve_extra(peer, k) for k in range(kv)])
 
     def finish(peer):
         for k in range(kv):

time: 46 us -> 45.8 us (level)
  no operation moved by 1% of the time
where the time goes in v5:
time: 45.8 us; the launch traced here: 45.7 us
  Pallas kernels  42.3 us (92%)
  local copies, waits for them, and re-layouts  3.33 us (7%)
    pallas_call x1, Pallas kernels, on_device(): pl.pallas_call(functools.partial(kernel, n, kv, group), out_shape=jax.Sha...  42.3 us
    unnamed x5, local copies, waits for them, and re-layouts  2.16 us
    reshape x1, local copies, waits for them, and re-layouts, on_device(): return out.reshape(pairs, tokens, kv, width)  1.17 us

profile of v5, /device:TPU:0, one launch (start us, length us, event | category | flops | bytes accessed | tf_op | source)
XLA Modules:
  0.0 45.7 jit_solution(6541129154391044793)
XLA Ops:
  0.0 0.0 copy-start
  0.0 1.5 %copy.4 = bf16[128,8,2,256]{3,1,2,0:T(8,128)(2,1)S(1)} copy(bf16[128,8,2,256]{3,2,1,0:T(2,128)(2,1)} %bitcast.4) | data formatting | bytes 2097152
  1.5 0.0 copy-start.1
  1.5 0.0 copy-done
  1.5 0.6 %copy-done.1 = s32[16]{0:T(128)S(1)} copy-done((s32[16]{0:T(128)S(1)}, s32[16]{0:T(128)}, u32[]{:S(2)}) %copy-start.1) | copy-done | bytes 88
  2.2 42.3 %shard_map.37 = bf16[4,32,2048]{2,1,0:T(8,128)(2,1)S(1)} custom-call(s32[16]{0:T(128)S(1)} %copy-done.1, bf16[4,32,2,1280]{3,2,1,0:T(2,128)(2,1)S(1)} %copy-done, bf16[1024,512]{1,0:T(8,128)(2,1)S(1)} %bitcast.3), custom_call_target="tpu_custom_call" | custom-call | flops 2147483648 | bytes 4194304 | tf_op jit(solution)/shard_map/pallas_call | solution.py:226
  44.5 1.2 %reshape.7 = bf16[4,32,2,1024]{3,2,1,0:T(2,128)(2,1)} reshape(bf16[4,32,2048]{2,1,0:T(8,128)(2,1)S(1)} %shard_map.37) | data formatting | bytes 1048576 | tf_op jit(solution)/shard_map/reshape | solution.py:247
Async XLA Ops:
  0.0 1.5 %copy-start = (bf16[4,32,2,1280]{3,2,1,0:T(2,128)(2,1)S(1)}, bf16[4,32,2,1280]{3,2,1,0:T(2,128)(2,1)}, u32[]{:S(2)}) copy-start(bf16[4,32,2,1280]{3,2,1,0:T(2,128)(2,1)} %rows_ref.1) | copy-start | bytes 1966084
  1.5 0.7 %copy-start.1 = (s32[16]{0:T(128)S(1)}, s32[16]{0:T(128)}, u32[]{:S(2)}) copy-start(s32[16]{0:T(128)} %clips_ref.1) | copy-start | bytes 196
